TPU v7x, 32 devices: a whole 2x2x4 slice. The times are simulated.
32 devices in a mesh: row: 8 (over y, x, core), col: 4 (over z).
Axes of the slice: x: 2, y: 2, z: 4, core: 2. Of those that a mesh axis runs over, the one named last changes fastest.
Arguments:
- p_blocks: bfloat16 [1536, 128, 128], P(('row', 'col')), may hold values from -6 to 6
- p_positions: int32 [1536], P(('row', 'col')), may hold values from 0 to 127, as said below
- h_blocks: bfloat16 [32, 128, 128], P('col'), may hold values from -0.1875 to 0.1875
- h_rows: int32 [32], replicated, may hold values from 0 to 63, as said below
- keep_mask: int32 [64, 4], P(('row', 'col')), may hold values 0 or 1
- owner_ids: int32 [64, 4, 1], P(('row', 'col')), may hold values from 0 to 7; in each aligned block of 8 rows (0 to 7, 8 to 15, ..., all dimensions but the last counted through in order) at most 2 rows name the same one
Outputs:
- owned: bfloat16 [256, 2, 128, 128], P(('row', 'col'))
Inputs may be any that keep to these rules, and one draw needn't show every extreme that they name: `p_positions`: within each group of 48 entries no value repeats. `h_rows`: within each group of 8 entries no value repeats. `owner_ids`: among the 8 blocks of one group of 2 block rows no owner appears more than 2 times.
All inputs are finite; a program needn't handle non-finite values. No bound on the sum of `keep_mask` on one device may be relied on, other than what follows from the above.
Results may differ from a plain program's by a relative error of at most 0.012.
Values may be sent and summed in bfloat16 or wider, within the bound.
A program may use at most 64 MiB of HBM per device.

v0:
```python
import jax
import jax.numpy as jnp
from jax import lax
from jax.sharding import PartitionSpec as P

RB = 2
KB = 64
SEND_CAP = 2


def shifted(value, axis, steps):
    count = lax.axis_size(axis)
    pairs = [(source, (source + steps) % count) for source in range(count)]
    return lax.ppermute(value, axis, pairs)


def advance(panel_blocks):
    return shifted(panel_blocks, "col", 1)


def local(p_blocks, p_positions, h_blocks, h_rows, keep_mask, owner_ids):
    cycle_size = lax.axis_size("col")
    owner_count = lax.axis_size("row")
    position = lax.axis_index("col")
    block_size = p_blocks.shape[-1]
    listed = h_blocks.shape[0]
    anchor = jnp.int32(0)
    slot_ids = p_positions % KB * RB + p_positions // KB
    dense_panel = (
        jnp.zeros((KB * RB, block_size, block_size), jnp.bfloat16).at[slot_ids].set(p_blocks)
    )
    dense_panel = dense_panel.reshape(KB, RB, block_size, block_size)

    def panel_term(panel_blocks, column):
        inner_rows = lax.dynamic_slice_in_dim(h_rows, column * listed, listed)
        columns = jnp.take(dense_panel, inner_rows, axis=0)
        return jnp.einsum(
            "nrab,nbc->rac", columns, panel_blocks, preferred_element_type=jnp.float32
        )

    def store_panel(totals, product, column):
        return lax.dynamic_update_slice(
            totals, product.astype(jnp.bfloat16)[:, None], (anchor, column, anchor, anchor)
        )

    totals = jnp.zeros((RB, cycle_size, block_size, block_size), jnp.bfloat16)
    totals = store_panel(totals, panel_term(h_blocks, position), position)

    def single_turn(turn_index, state):
        running, current = state
        current = advance(current)
        column = (position - turn_index) % cycle_size
        return (store_panel(running, panel_term(current, column), column), current)

    totals, current = lax.fori_loop(1, cycle_size, single_turn, (totals, h_blocks))
    kept_blocks = jnp.where(keep_mask[:, :, None, None] == 1, totals, jnp.zeros_like(totals))
    kept_blocks = kept_blocks.reshape(-1, block_size, block_size)
    target_owner = owner_ids.reshape(-1)
    onehot = (target_owner[:, None] == jnp.arange(owner_count, dtype=jnp.int32)[None, :]).astype(
        jnp.int32
    )
    rank_of = jnp.sum((jnp.cumsum(onehot, axis=0) - onehot) * onehot, axis=1)
    slot_match = (rank_of[:, None] == jnp.arange(SEND_CAP, dtype=jnp.int32)[None, :]).astype(
        jnp.int32
    )
    selector = (onehot[:, :, None] * slot_match[:, None, :]).astype(jnp.bfloat16)
    outgoing = jnp.einsum(
        "bos,bxy->osxy", selector, kept_blocks, preferred_element_type=jnp.float32
    ).astype(jnp.bfloat16)
    return lax.all_to_all(outgoing, "row", split_axis=0, concat_axis=0, tiled=True)


def solution(mesh):
    return jax.shard_map(
        local,
        mesh=mesh,
        in_specs=(
            P(("row", "col"), None, None),
            P(("row", "col")),
            P("col", None, None),
            P(),
            P(("row", "col"), None),
            P(("row", "col"), None, None),
        ),
        out_specs=P(("row", "col"), None, None, None),
        check_vma=False,
    )
```

profile of v0, /device:TPU:0, one launch (start us, length us, event | category | flops | bytes accessed | tf_op | source)
XLA Modules:
  0.0 62.7 jit_solution(13046721041754073492)
XLA Ops:
  0.0 1.1 %copy.46 = bf16[8,128,128]{2,1,0:T(8,128)(2,1)S(1)} copy(bf16[8,128,128]{2,1,0:T(8,128)(2,1)} %param.12) | data formatting | bytes 524288
  1.1 0.7 %compare_and_fusion.1 = (pred[8]{0:T(512)(128)(4,1)S(1)}, s32[8]{0:T(128)S(1)}) fusion(s32[32]{0:T(128)} %param.13, s32[]{:T(128)S(6)} %select_n.74), kind=kLoop, calls=%fused_computation.37 | loop fusion | flops 48 | bytes 76 | tf_op jit(solution)/shard_map/jit(_take)/and | solution.py:36
  1.8 0.7 %compare_select_fusion.2 = s32[48]{0:T(128)S(1)} fusion(s32[48]{0:T(128)} %param.11), kind=kLoop, calls=%fused_computation.36 | loop fusion | flops 1152 | bytes 384 | tf_op jit(solution)/shard_map/select_n | solution.py:30
  2.5 0.7 %broadcast_compare_fusion = pred[2,4]{1,0:T(4,128)(4,1)S(1)} fusion(s32[2,4]{1,0:T(2,128)} %param.14), kind=kLoop, calls=%fused_computation.46 | loop fusion | flops 8 | bytes 40 | tf_op jit(solution)/shard_map/eq | solution.py:56
  3.2 0.6 broadcast.98
  3.8 1.4 %reduce.3 = s32[2,4]{1,0:T(2,128)S(1)} reduce(s32[2,4,1]{1,2,0:T(1,128)} %param.15, s32[]{:T(128)} %broadcast.98), dimensions={2}, to_apply=%param.15.reduce_sub_computation.3 | reduce | bytes 68 | tf_op args[5]
  5.4 3.0 %broadcast_in_dim.43 = bf16[128,128,128]{2,1,0:T(8,128)(2,1)} broadcast(bf16[]{:T(256)} %constant.117.clone.1), dimensions={} | broadcast | bytes 4194306 | tf_op jit(solution)/shard_map/broadcast_in_dim | solution.py:30
  8.4 6.6 %scatter_fusion = bf16[128,128,128]{2,1,0:T(8,128)(2,1)} fusion(bf16[128,128,128]{2,1,0:T(8,128)(2,1)} %broadcast_in_dim.43, s32[48]{0:T(128)S(1)} %compare_select_fusion.2, bf16[48,128,128]{2,1,0:T(8,128)(2,1)S(1)} %copy-done), kind=kCustom, calls=%fused_computation.2 | custom fusion | bytes 4718784 | tf_op jit(solution)/shard_map/scatter | solution.py:30
  15.0 2.8 %gather_fusion.1 = bf16[8,2,128,128]{3,2,1,0:T(8,128)(2,1)S(1)} fusion(bf16[64,2,128,128]{3,2,1,0:T(8,128)(2,1)} %bitcast.55, s32[1024]{0:T(1024)S(1)} %pad_clamp_fusion.1), kind=kCustom, calls=%fused_computation.1.clone | custom fusion | bytes 1048608 | tf_op jit(solution)/shard_map/jit(_take)/gather | solution.py:36
  17.9 0.4 fusion.10
  18.2 30.5 %while.17 = (s32[]{:T(128)}, bf16[2,4,128,128]{3,2,1,0:T(8,128)(2,1)S(1)}, bf16[8,128,128]{2,1,0:T(8,128)(2,1)S(1)}, s32[]{:T(128)}, s32[32]{0:T(128)S(1)}, /*in...) while((s32[]{:T(128)}, ...), condition=%wide.region_4.6_spmd, body=%wide.region_3.5_spmd.sunk | while | flops 67404864 | bytes 3478518 | solution.py:55
  18.3 3.2 %collective-permute-start = (bf16[8,128,128]{2,1,0:T(8,128)(2,1)S(1)}, bf16[8,128,128]{2,1,0:T(8,128)(2,1)S(1)}, u32[]{:S(2)}, u32[]{:S(2)}) collective-permute-start(bf16[8,128,128]{2,1,0:T(8,128)(2,1)S(1)} %get-tuple-element.245), channel_id=1, source_target_pairs={{0,1},{1,2},{2,3},{3,0},{4,5},{5,6},{6,7},{7,4},{8,9},{9,10},{10,1... | collective-permute-start | bytes 786440 | tf_op jit(solution)/shard_map/while/body/eval_jaxpr/ppermute | solution.py:14
  21.5 2.8 %gather_fusion = bf16[8,2,128,128]{3,2,1,0:T(8,128)(2,1)S(1)} fusion(bf16[64,2,128,128]{3,2,1,0:T(8,128)(2,1)} %get-tuple-element.260, s32[1024]{0:T(1024)S(1)} %pad_clamp_fusion.3), kind=kCustom, calls=%fused_computation.clone.clone.1 | custom fusion | bytes 1048608 | tf_op jit(solution)/shard_map/while/body/eval_jaxpr/jit(_take)/gather | solution.py:36
  24.3 5.3 %collective-permute-done = bf16[8,128,128]{2,1,0:T(8,128)(2,1)S(1)} collective-permute-done((bf16[8,128,128]{2,1,0:T(8,128)(2,1)S(1)}, bf16[8,128,128]{2,1,0:T(8,128)(2,1)S(1)}, u32[]{:S(2)}, u32[]{:S(2)}) %collective-permute-start) | collective-permute-done | bytes 262176 | tf_op jit(solution)/shard_map/while/body/eval_jaxpr/ppermute | solution.py:14
  29.7 0.4 fusion.30
  30.3 2.8 %gather_fusion = bf16[8,2,128,128]{3,2,1,0:T(8,128)(2,1)S(1)} fusion(bf16[64,2,128,128]{3,2,1,0:T(8,128)(2,1)} %get-tuple-element.260, s32[1024]{0:T(1024)S(1)} %pad_clamp_fusion.3), kind=kCustom, calls=%fused_computation.clone.clone.1 | custom fusion | bytes 1048608 | tf_op jit(solution)/shard_map/while/body/eval_jaxpr/jit(_take)/gather | solution.py:36
  33.1 6.3 %collective-permute-done = bf16[8,128,128]{2,1,0:T(8,128)(2,1)S(1)} collective-permute-done((bf16[8,128,128]{2,1,0:T(8,128)(2,1)S(1)}, bf16[8,128,128]{2,1,0:T(8,128)(2,1)S(1)}, u32[]{:S(2)}, u32[]{:S(2)}) %collective-permute-start) | collective-permute-done | bytes 262176 | tf_op jit(solution)/shard_map/while/body/eval_jaxpr/ppermute | solution.py:14
  39.5 0.4 fusion.30
  40.1 2.8 %gather_fusion = bf16[8,2,128,128]{3,2,1,0:T(8,128)(2,1)S(1)} fusion(bf16[64,2,128,128]{3,2,1,0:T(8,128)(2,1)} %get-tuple-element.260, s32[1024]{0:T(1024)S(1)} %pad_clamp_fusion.3), kind=kCustom, calls=%fused_computation.clone.clone.1 | custom fusion | bytes 1048608 | tf_op jit(solution)/shard_map/while/body/eval_jaxpr/jit(_take)/gather | solution.py:36
  42.9 5.4 %collective-permute-done = bf16[8,128,128]{2,1,0:T(8,128)(2,1)S(1)} collective-permute-done((bf16[8,128,128]{2,1,0:T(8,128)(2,1)S(1)}, bf16[8,128,128]{2,1,0:T(8,128)(2,1)S(1)}, u32[]{:S(2)}, u32[]{:S(2)}) %collective-permute-start) | collective-permute-done | bytes 262176 | tf_op jit(solution)/shard_map/while/body/eval_jaxpr/ppermute | solution.py:14
  48.3 0.4 fusion.30
  48.8 0.3 convolution_convert_fusion
  49.2 12.7 %all_to_all.5 = bf16[8,2,128,128]{3,2,1,0:T(8,128)(2,1)S(1)} all-to-all(bf16[8,2,128,128]{3,2,1,0:T(8,128)(2,1)S(1)} %copy.22), channel_id=1, replica_groups=mesh['row'=8,'col'=4] {'row'}, dimensions={0} | all-to-all | bytes 1048576 | tf_op jit(solution)/shard_map/all_to_all | solution.py:70
  61.9 0.8 %copy.47 = bf16[8,2,128,128]{3,2,1,0:T(8,128)(2,1)} copy(bf16[8,2,128,128]{3,2,1,0:T(8,128)(2,1)S(1)} %all_to_all.5) | data formatting | bytes 1048576
  (24 shorter events, 0.9 us)
Async XLA Ops:
  0.0 8.4 %copy-start = (bf16[48,128,128]{2,1,0:T(8,128)(2,1)S(1)}, bf16[48,128,128]{2,1,0:T(8,128)(2,1)}, u32[]{:S(2)}) copy-start(bf16[48,128,128]{2,1,0:T(8,128)(2,1)} %param.10) | copy-start | bytes 4718596
  8.4 9.8 %copy-start.1 = (s32[32]{0:T(128)S(1)}, s32[32]{0:T(128)}, u32[]{:S(2)}) copy-start(s32[32]{0:T(128)} %param.13) | copy-start | bytes 388
  18.3 11.4 %collective-permute-start = (bf16[8,128,128]{2,1,0:T(8,128)(2,1)S(1)}, bf16[8,128,128]{2,1,0:T(8,128)(2,1)S(1)}, u32[]{:S(2)}, u32[]{:S(2)}) collective-permute-start(bf16[8,128,128]{2,1,0:T(8,128)(2,1)S(1)} %get-tuple-element.245), channel_id=1, source_target_pairs={{0,1},{1,2},{2,3},{3,0},{4,5},{5,6},{6,7},{7,4},{8,9},{9,10},{10,1... | collective-permute-start | bytes 786440 | tf_op jit(solution)/shard_map/while/body/eval_jaxpr/ppermute | solution.py:14
  30.1 9.4 %collective-permute-start = (bf16[8,128,128]{2,1,0:T(8,128)(2,1)S(1)}, bf16[8,128,128]{2,1,0:T(8,128)(2,1)S(1)}, u32[]{:S(2)}, u32[]{:S(2)}) collective-permute-start(bf16[8,128,128]{2,1,0:T(8,128)(2,1)S(1)} %get-tuple-element.245), channel_id=1, source_target_pairs={{0,1},{1,2},{2,3},{3,0},{4,5},{5,6},{6,7},{7,4},{8,9},{9,10},{10,1... | collective-permute-start | bytes 786440 | tf_op jit(solution)/shard_map/while/body/eval_jaxpr/ppermute | solution.py:14
  39.9 8.4 %collective-permute-start = (bf16[8,128,128]{2,1,0:T(8,128)(2,1)S(1)}, bf16[8,128,128]{2,1,0:T(8,128)(2,1)S(1)}, u32[]{:S(2)}, u32[]{:S(2)}) collective-permute-start(bf16[8,128,128]{2,1,0:T(8,128)(2,1)S(1)} %get-tuple-element.245), channel_id=1, source_target_pairs={{0,1},{1,2},{2,3},{3,0},{4,5},{5,6},{6,7},{7,4},{8,9},{9,10},{10,1... | collective-permute-start | bytes 786440 | tf_op jit(solution)/shard_map/while/body/eval_jaxpr/ppermute | solution.py:14
where the time goes:
time: 63.4 us; the launch traced here: 62.7 us
  local copies, waits for them, and re-layouts  23.6 us (37%)
  waiting for transfers between devices  17.1 us (27%)
  blocking collectives  12.7 us (20%)
  other arithmetic  4.03 us (6%)
  starting transfers between devices  3.27 us (5%)
  matrix products  1.78 us (3%)
    ppermute x3, waiting for transfers between devices, shifted(): return lax.ppermute(value, axis, pairs)  17.1 us
    all_to_all x1, blocking collectives, local(): lax.all_to_all(outgoing, 'row', split_axis=0, concat_axis=0, tiled=True)  12.7 us
    gather x4, local copies, waits for them, and re-layouts, panel_term(): columns = jnp.take(dense_panel, inner_rows, axis=0)  11.3 us
    scatter x1, local copies, waits for them, and re-layouts, local(): jnp.zeros((KB * RB, block_size, block_size), jnp.bfloat16).at[slot_ids]  6.57 us
    ppermute x3, starting transfers between devices, shifted(): return lax.ppermute(value, axis, pairs)  3.27 us
    broadcast_in_dim x1, local copies, waits for them, and re-layouts, local(): jnp.zeros((KB * RB, block_size, block_size), jnp.bfloat16).at[slot_ids]  2.97 us
    unnamed x7, local copies, waits for them, and re-layouts  2.46 us
    dot_general x4, matrix products, panel_term(): jnp.einsum('nrab,nbc->rac', columns, panel_blocks, preferred_element_type...  1.49 us
  transfers between devices with their start and end apart: 3, of which 3 were waited for; matrix products, arithmetic and copies ran while one was open for 14% of the time, Pallas kernels for 0%

commit v1 on v0

v1 whole, which is shorter than its diff:
```python
import functools

import jax
import jax.numpy as jnp
from jax import lax
from jax.experimental import pallas as pl
from jax.experimental.pallas import tpu as pltpu
from jax.sharding import PartitionSpec as P

KB = 64
SEND_CAP = 2
LANES = 128
UNROLL = 64
MESH = pl.DeviceIdType.MESH


def repeat(count, body, init=None):
    if count <= UNROLL:
        for i in range(count):
            init = body(i, init)
        return init
    return lax.fori_loop(0, count, body, init)


def flip(value, stride):
    bit = lax.rem(lax.div(value, stride), 2)
    return value + stride * (1 - 2 * bit)


def xor(value, mask):
    bit = 1
    while bit <= mask:
        if mask & bit:
            value = flip(value, jnp.int32(bit))
        bit *= 2
    return value


def kernel(
    rows, cols, pos_ref, hrow_ref, keep_ref, owner_ref, p_ref, h_ref, out_ref,
    pv, hall, kept, outgoing, table, stable,
    local_sem, move_send, move_recv, core_send, core_recv, deal_send, deal_recv,
):
    me_r, me_c = lax.axis_index("row"), lax.axis_index("col")
    core = lax.rem(me_r, 2)
    listed_p = p_ref.shape[0]
    block = p_ref.shape[-1]
    rb, ncb = keep_ref.shape
    blocks = rb * ncb
    listed_h = hrow_ref.shape[0] // cols
    dims = rows.bit_length() - 2
    places = 2**dims
    power = cols & (cols - 1) == 0

    def target(step):
        return xor(me_c, step) if power else lax.rem(me_c + step, cols)

    def origin(step):
        return xor(me_c, step) if power else lax.rem(me_c + cols - step, cols)

    strides = []
    for i in range(dims):
        first, second = 2 ** (dims - i), 2 ** (i + 1)
        strides.append(first + core * (second - first))
    pieces = [me_r]
    for stride in strides:
        pieces = pieces + [flip(piece, stride) for piece in pieces]
    partner = flip(me_r, jnp.int32(1))

    p_copy = pltpu.make_async_copy(p_ref, pv.at[pl.ds(0, listed_p)], local_sem.at[0])
    h_copy = pltpu.make_async_copy(h_ref, hall.at[me_c], local_sem.at[1])
    p_copy.start()
    h_copy.start()

    barrier = pltpu.get_barrier_semaphore()
    for step in range(1, cols):
        pl.semaphore_signal(barrier, inc=1, device_id=(me_r, target(step)), device_id_type=MESH)
    for step in range(1, rows):
        pl.semaphore_signal(barrier, inc=1, device_id=(xor(me_r, step), me_c), device_id_type=MESH)
    pl.semaphore_wait(barrier, cols + rows - 2)

    def first_copy(step):
        return pltpu.make_async_remote_copy(
            src_ref=h_ref.at[me_r], dst_ref=hall.at[me_c, me_r],
            send_sem=move_send.at[step, 0], recv_sem=move_recv.at[step, 0],
            device_id=(me_r, target(step)), device_id_type=MESH,
        )

    def plane_copy(step, place, onto, to_row, sends, recvs):
        piece = hall.at[origin(step), pieces[place]]
        return pltpu.make_async_remote_copy(
            src_ref=piece, dst_ref=piece,
            send_sem=sends.at[step, onto], recv_sem=recvs.at[step, onto],
            device_id=(to_row, me_c), device_id_type=MESH,
        )

    def core_copy(step, place):
        return plane_copy(step, place, place, partner, core_send, core_recv)

    for step in range(1, cols):
        first_copy(step).start()

    width = table.shape[-1]
    lane = lax.broadcasted_iota(jnp.int32, (8, width), 1)
    line = lax.broadcasted_iota(jnp.int32, (8, width), 0)
    wanted = repeat(
        hrow_ref.shape[0], lambda m, held: jnp.where(lane == m, hrow_ref[m], held),
        jnp.full((8, width), -1, jnp.int32),
    )
    wanted = jnp.where(wanted < 0, -1, wanted + line * KB)
    table[0] = repeat(
        listed_p, lambda q, held: jnp.where(wanted == pos_ref[q], q, held),
        jnp.full((8, width), listed_p, jnp.int32),
    )
    filled = jnp.full((8, width), blocks, jnp.int32)
    count = jnp.zeros((8, width), jnp.int32)
    for b in range(blocks):
        r, j = b // ncb, b % ncb
        hit = lane == owner_ref[r, j, 0]
        taken = jnp.where(keep_ref[r, j] == 1, b, blocks)
        filled = jnp.where(hit & (count == line), taken, filled)
        count = count + hit.astype(jnp.int32)
    table[1] = filled
    t_copy = pltpu.make_async_copy(table, stable, local_sem.at[2])
    t_copy.start()
    pv[listed_p] = jnp.zeros((block, block), jnp.bfloat16)
    kept[blocks] = jnp.zeros((block, block), jnp.bfloat16)
    t_copy.wait()

    def multiply(column):
        sides = []
        for r in range(rb):
            sides.append(jnp.concatenate(
                [pv[stable[0, r, column * listed_h + n]] for n in range(listed_h)], axis=1
            ))
        panel = hall[column].reshape(listed_h * block, block)
        product = jnp.dot(
            jnp.concatenate(sides, axis=0), panel, preferred_element_type=jnp.float32
        ).astype(jnp.bfloat16)
        for r in range(rb):
            kept[r * ncb + column] = product[r * block:(r + 1) * block]

    for step in range(1, cols):
        first_copy(step).wait_recv()
        for i in range(dims):
            plane_copy(step, 0, 2**i, flip(me_r, strides[i]), move_send, move_recv).start()
        core_copy(step, 0).start()
    p_copy.wait()
    h_copy.wait()
    multiply(me_c)
    for place in range(1, places):
        made = place.bit_length() - 1
        for step in range(1, cols):
            plane_copy(step, place, place, me_r, move_send, move_recv).wait_recv()
            for i in range(made + 1, dims):
                plane_copy(
                    step, place, 2**i + place, flip(me_r, strides[i]), move_send, move_recv
                ).start()
            core_copy(step, place).start()
    for step in range(1, cols):
        for place in range(places):
            other = flip(pieces[place], jnp.int32(1))
            pltpu.make_async_remote_copy(
                src_ref=hall.at[origin(step), other], dst_ref=hall.at[origin(step), other],
                send_sem=core_send.at[step, place], recv_sem=core_recv.at[step, place],
                device_id=(partner, me_c), device_id_type=MESH,
            ).wait_recv()
        multiply(origin(step))

    def deal(step):
        owner = xor(me_r, step)
        return pltpu.make_async_remote_copy(
            src_ref=outgoing.at[owner], dst_ref=out_ref.at[me_r],
            send_sem=deal_send.at[step], recv_sem=deal_recv.at[step],
            device_id=(owner, me_c), device_id_type=MESH,
        )

    for step in range(rows - 1, -1, -1):
        owner = xor(me_r, step)
        for s in range(SEND_CAP):
            outgoing[owner, s] = kept[stable[1, s, owner]]
        if step:
            deal(step).start()
    own = pltpu.make_async_copy(outgoing.at[me_r], out_ref.at[me_r], local_sem.at[3])
    own.start()
    for step in range(1, cols):
        first_copy(step).wait_send()
        for place in range(places):
            if place:
                plane_copy(step, 0, place, me_r, move_send, move_recv).wait_send()
            core_copy(step, place).wait_send()
    for step in range(rows - 1, 0, -1):
        deal(step).wait_send()
        deal(step).wait_recv()
    own.wait()


def local(rows, cols, p_blocks, p_positions, h_blocks, h_rows, keep_mask, owner_ids):
    listed_p, block = p_blocks.shape[:2]
    listed_h = h_blocks.shape[0]
    blocks = keep_mask.size
    depth = listed_h * block // rows
    places = rows // 2
    width = -(-max(h_rows.shape[0], rows) // LANES) * LANES
    smem = pl.BlockSpec(memory_space=pltpu.SMEM)
    anywhere = pl.BlockSpec(memory_space=pl.ANY)
    dma = pltpu.SemaphoreType.DMA
    return pl.pallas_call(
        functools.partial(kernel, rows, cols),
        out_shape=jax.ShapeDtypeStruct((rows, SEND_CAP, block, block), jnp.bfloat16),
        in_specs=[smem] * 4 + [anywhere] * 2,
        out_specs=anywhere,
        scratch_shapes=[
            pltpu.VMEM((listed_p + 1, block, block), jnp.bfloat16),
            pltpu.VMEM((cols, rows, depth, block), jnp.bfloat16),
            pltpu.VMEM((blocks + 1, block, block), jnp.bfloat16),
            pltpu.VMEM((rows, SEND_CAP, block, block), jnp.bfloat16),
            pltpu.VMEM((2, 8, width), jnp.int32),
            pltpu.SMEM((2, 8, width), jnp.int32),
            dma((4,)),
            dma((cols, places)),
            dma((cols, places)),
            dma((cols, places)),
            dma((cols, places)),
            dma((rows,)),
            dma((rows,)),
        ],
        compiler_params=pltpu.CompilerParams(
            collective_id=0, has_side_effects=True, vmem_limit_bytes=32 * 1024 * 1024
        ),
    )(
        p_positions, h_rows, keep_mask, owner_ids, p_blocks,
        h_blocks.reshape(rows, depth, block),
    )


def solution(mesh):
    return jax.shard_map(
        functools.partial(local, mesh.shape["row"], mesh.shape["col"]),
        mesh=mesh,
        in_specs=(
            P(("row", "col"), None, None),
            P(("row", "col")),
            P("col", None, None),
            P(),
            P(("row", "col"), None),
            P(("row", "col"), None, None),
        ),
        out_specs=P(("row", "col"), None, None, None),
        check_vma=False,
    )
```

time: 63.4 us -> 32.8 us (0.52)
  Pallas kernels: 0 us -> 26.6 us
  local copies, waits for them, and re-layouts: 23.6 us -> 5.91 us
  waiting for transfers between devices: 17.1 us -> 0 us
  blocking collectives: 12.7 us -> 0 us
  other arithmetic: 4.03 us -> 0 us
  starting transfers between devices: 3.27 us -> 0 us
  matrix products: 1.78 us -> 0 us
    pallas_call x0 -> x1, Pallas kernels: none -> 26.6 us  [local(): pl.pallas_call(functools.partial(kernel, rows, cols), out_shape=jax.Shape...]
    ppermute x3 -> x0, waiting for transfers between devices: 17.1 us -> none  [shifted(): return lax.ppermute(value, axis, pairs)]
    all_to_all x1 -> x0, blocking collectives: 12.7 us -> none  [local(): lax.all_to_all(outgoing, 'row', split_axis=0, concat_axis=0, tiled=True)]
    gather x4 -> x0, local copies, waits for them, and re-layouts: 11.3 us -> none  [panel_term(): columns = jnp.take(dense_panel, inner_rows, axis=0)]
    scatter x1 -> x0, local copies, waits for them, and re-layouts: 6.57 us -> none  [local(): jnp.zeros((KB * RB, block_size, block_size), jnp.bfloat16).at[slot_ids]]
    unnamed x7 -> x12, local copies, waits for them, and re-layouts: 2.46 us -> 5.91 us
    ppermute x3 -> x0, starting transfers between devices: 3.27 us -> none  [shifted(): return lax.ppermute(value, axis, pairs)]
    broadcast_in_dim x1 -> x0, local copies, waits for them, and re-layouts: 2.97 us -> none  [local(): jnp.zeros((KB * RB, block_size, block_size), jnp.bfloat16).at[slot_ids]]
  transfers between devices with their start and end apart: 3 -> 0, of which waited for: 3 -> 0; matrix products, arithmetic and copies ran while one was open for 14% -> 0% of each run, Pallas kernels for 0% -> 0%
where the time goes in v1:
time: 32.8 us; the launch traced here: 32.5 us
  Pallas kernels  26.6 us (81%)
  local copies, waits for them, and re-layouts  5.91 us (18%)
    pallas_call x1, Pallas kernels, local(): pl.pallas_call(functools.partial(kernel, rows, cols), out_shape=jax.Shape...  26.6 us
    unnamed x12, local copies, waits for them, and re-layouts  5.91 us

profile of v1, /device:TPU:0, one launch (start us, length us, event | category | flops | bytes accessed | tf_op | source)
XLA Modules:
  0.0 32.5 jit_solution(17703551264404964662)
XLA Ops:
  0.0 0.8 %copy.7.owner_ref = s32[2,4,1]{2,1,0:T(4,128)S(1)} copy(s32[2,4,1]{1,2,0:T(1,128)} %param.11) | data formatting | bytes 64 | tf_op args[5]
  0.8 0.0 copy-start
  0.8 1.4 %copy-done = bf16[48,128,128]{2,1,0:T(8,128)(2,1)S(1)} copy-done((bf16[48,128,128]{2,1,0:T(8,128)(2,1)S(1)}, bf16[48,128,128]{2,1,0:T(8,128)(2,1)}, u32[]{:S(2)}) %copy-start) | copy-done | bytes 1572888
  2.2 0.0 copy-start.1
  2.2 0.9 %copy-done.1 = bf16[8,128,128]{2,1,0:T(8,128)(2,1)S(1)} copy-done((bf16[8,128,128]{2,1,0:T(8,128)(2,1)S(1)}, bf16[8,128,128]{2,1,0:T(8,128)(2,1)}, u32[]{:S(2)}) %copy-start.1) | copy-done | bytes 262168
  3.1 0.0 copy-start.2
  3.1 0.7 %copy-done.2 = s32[2,4]{1,0:T(2,128)S(1)} copy-done((s32[2,4]{1,0:T(2,128)S(1)}, s32[2,4]{1,0:T(2,128)}, u32[]{:S(2)}) %copy-start.2) | copy-done | bytes 56
  3.8 0.0 copy-start.3
  3.8 0.7 %copy-done.3 = s32[48]{0:T(128)S(1)} copy-done((s32[48]{0:T(128)S(1)}, s32[48]{0:T(128)}, u32[]{:S(2)}) %copy-start.3) | copy-done | bytes 216
  4.5 0.0 copy-start.4
  4.5 0.7 %copy-done.4 = s32[32]{0:T(128)S(1)} copy-done((s32[32]{0:T(128)S(1)}, s32[32]{0:T(128)}, u32[]{:S(2)}) %copy-start.4) | copy-done | bytes 152
  5.1 26.6 %shard_map.64 = bf16[8,2,128,128]{3,2,1,0:T(8,128)(2,1)S(1)} custom-call(s32[48]{0:T(128)S(1)} %copy-done.3, s32[32]{0:T(128)S(1)} %copy-done.4, s32[2,4]{1,0:T(2,128)S(1)} %copy-done.2, s32[2,4,1]{2,1,0:T(4,128)S(1)} %copy.7.owner_ref, bf16[48,128,128]{2,1,0:T(8,128)(2,1)S(1)} %copy-done, bf16[8,128,128]{2,1,0:T(8,128)(2,1)S(1)} %copy-done.1), custom_call_target="tpu_custom_call" | custom-call | tf_op jit(solution)/shard_map/pallas_call | solution.py:208
  31.7 0.8 %copy.9 = bf16[8,2,128,128]{3,2,1,0:T(8,128)(2,1)} copy(bf16[8,2,128,128]{3,2,1,0:T(8,128)(2,1)S(1)} %shard_map.64) | data formatting | bytes 1048576
Async XLA Ops:
  0.8 1.4 %copy-start = (bf16[48,128,128]{2,1,0:T(8,128)(2,1)S(1)}, bf16[48,128,128]{2,1,0:T(8,128)(2,1)}, u32[]{:S(2)}) copy-start(bf16[48,128,128]{2,1,0:T(8,128)(2,1)} %p_ref.1) | copy-start | bytes 4718596
  2.2 0.9 %copy-start.1 = (bf16[8,128,128]{2,1,0:T(8,128)(2,1)S(1)}, bf16[8,128,128]{2,1,0:T(8,128)(2,1)}, u32[]{:S(2)}) copy-start(bf16[8,128,128]{2,1,0:T(8,128)(2,1)} %h_ref.1) | copy-start | bytes 786436
  3.1 0.7 %copy-start.2 = (s32[2,4]{1,0:T(2,128)S(1)}, s32[2,4]{1,0:T(2,128)}, u32[]{:S(2)}) copy-start(s32[2,4]{1,0:T(2,128)} %keep_ref.1) | copy-start | bytes 100
  3.8 0.7 %copy-start.3 = (s32[48]{0:T(128)S(1)}, s32[48]{0:T(128)}, u32[]{:S(2)}) copy-start(s32[48]{0:T(128)} %pos_ref.1) | copy-start | bytes 580
  4.5 0.7 %copy-start.4 = (s32[32]{0:T(128)S(1)}, s32[32]{0:T(128)}, u32[]{:S(2)}) copy-start(s32[32]{0:T(128)} %hrow_ref.1) | copy-start | bytes 388

commit v2 on v1

--- a/solution.py
+++ b/solution.py
@@ -22,23 +22,18 @@
     return lax.fori_loop(0, count, body, init)
 
 
-def flip(value, stride):
-    bit = lax.rem(lax.div(value, stride), 2)
-    return value + stride * (1 - 2 * bit)
-
-
 def xor(value, mask):
     bit = 1
     while bit <= mask:
         if mask & bit:
-            value = flip(value, jnp.int32(bit))
+            value = value + bit * (1 - 2 * lax.rem(lax.div(value, bit), 2))
         bit *= 2
     return value
 
 
 def kernel(
-    rows, cols, pos_ref, hrow_ref, keep_ref, owner_ref, p_ref, h_ref, out_ref,
-    pv, hall, kept, outgoing, table, stable,
+    rows, cols, pos_in, hrow_in, keep_in, owner_in, p_ref, h_ref, out_ref,
+    pos_ref, hrow_ref, keep_ref, owner_ref, pv, hall, kept, outgoing, table, stable,
     local_sem, move_send, move_recv, core_send, core_recv, deal_send, deal_recv,
 ):
     me_r, me_c = lax.axis_index("row"), lax.axis_index("col")
@@ -61,22 +56,32 @@
     strides = []
     for i in range(dims):
         first, second = 2 ** (dims - i), 2 ** (i + 1)
-        strides.append(first + core * (second - first))
+        moves = [stride * (1 - 2 * lax.rem(lax.div(me_r, stride), 2)) for stride in (first, second)]
+        strides.append(moves[0] + core * (moves[1] - moves[0]))
     pieces = [me_r]
     for stride in strides:
-        pieces = pieces + [flip(piece, stride) for piece in pieces]
-    partner = flip(me_r, jnp.int32(1))
+        pieces = pieces + [piece + stride for piece in pieces]
+    toward = 1 - 2 * core
+    partner = me_r + toward
 
     p_copy = pltpu.make_async_copy(p_ref, pv.at[pl.ds(0, listed_p)], local_sem.at[0])
     h_copy = pltpu.make_async_copy(h_ref, hall.at[me_c], local_sem.at[1])
-    p_copy.start()
-    h_copy.start()
+    small = [
+        pltpu.make_async_copy(given, held, local_sem.at[4 + i])
+        for i, (given, held) in enumerate((
+            (pos_in, pos_ref), (hrow_in, hrow_ref), (keep_in, keep_ref), (owner_in, owner_ref)
+        ))
+    ]
+    for copy in small:
+        copy.start()
 
     barrier = pltpu.get_barrier_semaphore()
     for step in range(1, cols):
         pl.semaphore_signal(barrier, inc=1, device_id=(me_r, target(step)), device_id_type=MESH)
     for step in range(1, rows):
         pl.semaphore_signal(barrier, inc=1, device_id=(xor(me_r, step), me_c), device_id_type=MESH)
+    h_copy.start()
+    p_copy.start()
     pl.semaphore_wait(barrier, cols + rows - 2)
 
     def first_copy(step):
@@ -99,6 +104,8 @@
 
     for step in range(1, cols):
         first_copy(step).start()
+    for copy in small:
+        copy.wait()
 
     width = table.shape[-1]
     lane = lax.broadcasted_iota(jnp.int32, (8, width), 1)
@@ -116,7 +123,7 @@
     count = jnp.zeros((8, width), jnp.int32)
     for b in range(blocks):
         r, j = b // ncb, b % ncb
-        hit = lane == owner_ref[r, j, 0]
+        hit = lane == owner_ref[r, 0, j]
         taken = jnp.where(keep_ref[r, j] == 1, b, blocks)
         filled = jnp.where(hit & (count == line), taken, filled)
         count = count + hit.astype(jnp.int32)
@@ -143,7 +150,7 @@
     for step in range(1, cols):
         first_copy(step).wait_recv()
         for i in range(dims):
-            plane_copy(step, 0, 2**i, flip(me_r, strides[i]), move_send, move_recv).start()
+            plane_copy(step, 0, 2**i, me_r + strides[i], move_send, move_recv).start()
         core_copy(step, 0).start()
     p_copy.wait()
     h_copy.wait()
@@ -154,12 +161,12 @@
             plane_copy(step, place, place, me_r, move_send, move_recv).wait_recv()
             for i in range(made + 1, dims):
                 plane_copy(
-                    step, place, 2**i + place, flip(me_r, strides[i]), move_send, move_recv
+                    step, place, 2**i + place, me_r + strides[i], move_send, move_recv
                 ).start()
             core_copy(step, place).start()
     for step in range(1, cols):
         for place in range(places):
-            other = flip(pieces[place], jnp.int32(1))
+            other = pieces[place] + toward
             pltpu.make_async_remote_copy(
                 src_ref=hall.at[origin(step), other], dst_ref=hall.at[origin(step), other],
                 send_sem=core_send.at[step, place], recv_sem=core_recv.at[step, place],
@@ -202,22 +209,26 @@
     depth = listed_h * block // rows
     places = rows // 2
     width = -(-max(h_rows.shape[0], rows) // LANES) * LANES
-    smem = pl.BlockSpec(memory_space=pltpu.SMEM)
+    hbm = pl.BlockSpec(memory_space=pltpu.HBM)
     anywhere = pl.BlockSpec(memory_space=pl.ANY)
     dma = pltpu.SemaphoreType.DMA
     return pl.pallas_call(
         functools.partial(kernel, rows, cols),
         out_shape=jax.ShapeDtypeStruct((rows, SEND_CAP, block, block), jnp.bfloat16),
-        in_specs=[smem] * 4 + [anywhere] * 2,
+        in_specs=[hbm] * 6,
         out_specs=anywhere,
         scratch_shapes=[
+            pltpu.SMEM(p_positions.shape, jnp.int32),
+            pltpu.SMEM(h_rows.shape, jnp.int32),
+            pltpu.SMEM(keep_mask.shape, jnp.int32),
+            pltpu.SMEM((keep_mask.shape[0], 1, keep_mask.shape[1]), jnp.int32),
             pltpu.VMEM((listed_p + 1, block, block), jnp.bfloat16),
             pltpu.VMEM((cols, rows, depth, block), jnp.bfloat16),
             pltpu.VMEM((blocks + 1, block, block), jnp.bfloat16),
             pltpu.VMEM((rows, SEND_CAP, block, block), jnp.bfloat16),
             pltpu.VMEM((2, 8, width), jnp.int32),
             pltpu.SMEM((2, 8, width), jnp.int32),
-            dma((4,)),
+            dma((8,)),
             dma((cols, places)),
             dma((cols, places)),
             dma((cols, places)),
@@ -226,10 +237,10 @@
             dma((rows,)),
         ],
         compiler_params=pltpu.CompilerParams(
-            collective_id=0, has_side_effects=True, vmem_limit_bytes=32 * 1024 * 1024
+            collective_id=0, has_side_effects=True, vmem_limit_bytes=56 * 1024 * 1024
         ),
     )(
-        p_positions, h_rows, keep_mask, owner_ids, p_blocks,
+        p_positions, h_rows, keep_mask, jnp.transpose(owner_ids, (0, 2, 1)), p_blocks,
         h_blocks.reshape(rows, depth, block),
     )
 

time: 32.8 us -> 28.1 us (0.86)
  local copies, waits for them, and re-layouts: 5.91 us -> 1.89 us
  Pallas kernels: 26.6 us -> 26.1 us
    unnamed x12 -> x1, local copies, waits for them, and re-layouts: 5.91 us -> 1.89 us
    pallas_call x1, Pallas kernels: 26.6 us -> 26.1 us  [local(): pl.pallas_call(functools.partial(kernel, rows, cols), out_shape=jax.Shape...]
where the time goes in v2:
time: 28.1 us; the launch traced here: 28 us
  Pallas kernels  26.1 us (93%)
  local copies, waits for them, and re-layouts  1.89 us (7%)
    pallas_call x1, Pallas kernels, local(): pl.pallas_call(functools.partial(kernel, rows, cols), out_shape=jax.Shape...  26.1 us
    unnamed x1, local copies, waits for them, and re-layouts  1.89 us

profile of v2, /device:TPU:0, one launch (start us, length us, event | category | flops | bytes accessed | tf_op | source)
XLA Modules:
  0.0 28.0 jit_solution(6150676617079072266)
XLA Ops:
  0.0 26.1 %shard_map.64 = bf16[8,2,128,128]{3,2,1,0:T(8,128)(2,1)} custom-call(s32[48]{0:T(128)} %pos_in.1, s32[32]{0:T(128)} %hrow_in.1, s32[2,4]{1,0:T(2,128)} %keep_in.1, s32[2,1,4]{2,1,0:T(1,128)} %bitcast.3, bf16[48,128,128]{2,1,0:T(8,128)(2,1)} %p_ref.1, bf16[8,128,128]{2,1,0:T(8,128)(2,1)} %h_ref.1), custom_call_target="tpu_custom_call" | custom-call | tf_op jit(solution)/shard_map/pallas_call | solution.py:215
  26.1 1.9 %copy.9 = bf16[8,2,128,128]{3,2,1,0:T(8,128)(2,1)} copy(bf16[8,2,128,128]{3,2,1,0:T(8,128)(2,1)} %shard_map.64) | data formatting | bytes 1048576

commit v3 on v2

--- a/solution.py
+++ b/solution.py
@@ -149,20 +149,15 @@
 
     for step in range(1, cols):
         first_copy(step).wait_recv()
-        for i in range(dims):
-            plane_copy(step, 0, 2**i, me_r + strides[i], move_send, move_recv).start()
+        for place in range(places - 1, 0, -1):
+            plane_copy(step, 0, place, pieces[place], move_send, move_recv).start()
         core_copy(step, 0).start()
     p_copy.wait()
     h_copy.wait()
     multiply(me_c)
-    for place in range(1, places):
-        made = place.bit_length() - 1
-        for step in range(1, cols):
+    for step in range(1, cols):
+        for place in range(1, places):
             plane_copy(step, place, place, me_r, move_send, move_recv).wait_recv()
-            for i in range(made + 1, dims):
-                plane_copy(
-                    step, place, 2**i + place, me_r + strides[i], move_send, move_recv
-                ).start()
             core_copy(step, place).start()
     for step in range(1, cols):
         for place in range(places):
@@ -214,7 +209,7 @@
     dma = pltpu.SemaphoreType.DMA
     return pl.pallas_call(
         functools.partial(kernel, rows, cols),
-        out_shape=jax.ShapeDtypeStruct((rows, SEND_CAP, block, block), jnp.bfloat16),
+        out_shape=pltpu.VMEM((rows, SEND_CAP, block, block), jnp.bfloat16),
         in_specs=[hbm] * 6,
         out_specs=anywhere,
         scratch_shapes=[
@@ -237,12 +232,14 @@
             dma((rows,)),
         ],
         compiler_params=pltpu.CompilerParams(
-            collective_id=0, has_side_effects=True, vmem_limit_bytes=56 * 1024 * 1024
+            collective_id=0, has_side_effects=True, vmem_limit_bytes=40 * 1024 * 1024
         ),
-    )(
-        p_positions, h_rows, keep_mask, jnp.transpose(owner_ids, (0, 2, 1)), p_blocks,
-        h_blocks.reshape(rows, depth, block),
-    )
+    )(*[
+        pltpu.with_memory_space_constraint(given, pltpu.HBM) for given in (
+            p_positions, h_rows, keep_mask, jnp.transpose(owner_ids, (0, 2, 1)), p_blocks,
+            h_blocks.reshape(rows, depth, block),
+        )
+    ])
 
 
 def solution(mesh):

time: 28.1 us -> 24.9 us (0.89)
  Pallas kernels: 26.1 us -> 24 us
  local copies, waits for them, and re-layouts: 1.89 us -> 0.8 us
    pallas_call x1, Pallas kernels: 26.1 us -> 24 us  [local(): pl.pallas_call(functools.partial(kernel, rows, cols), out_shape=pltpu.VME...]
    unnamed x1, local copies, waits for them, and re-layouts: 1.89 us -> 0.8 us
where the time goes in v3:
time: 24.9 us; the launch traced here: 24.8 us
  Pallas kernels  24 us (96%)
  local copies, waits for them, and re-layouts  0.8 us (3%)
    pallas_call x1, Pallas kernels, local(): pl.pallas_call(functools.partial(kernel, rows, cols), out_shape=pltpu.VME...  24 us
    unnamed x1, local copies, waits for them, and re-layouts  0.8 us

profile of v3, /device:TPU:0, one launch (start us, length us, event | category | flops | bytes accessed | tf_op | source)
XLA Modules:
  0.0 24.8 jit_solution(16474361290221373788)
XLA Ops:
  0.0 24.0 %shard_map.64 = bf16[8,2,128,128]{3,2,1,0:T(8,128)(2,1)S(1)} custom-call(s32[48]{0:T(128)} %pos_in.1, s32[32]{0:T(128)} %hrow_in.1, s32[2,4]{1,0:T(2,128)} %keep_in.1, s32[2,1,4]{2,1,0:T(1,128)} %bitcast.3, bf16[48,128,128]{2,1,0:T(8,128)(2,1)} %p_ref.1, bf16[8,128,128]{2,1,0:T(8,128)(2,1)} %h_ref.1), custom_call_target="tpu_custom_call" | custom-call | tf_op jit(solution)/shard_map/pallas_call | solution.py:210
  24.0 0.8 %copy.9 = bf16[8,2,128,128]{3,2,1,0:T(8,128)(2,1)} copy(bf16[8,2,128,128]{3,2,1,0:T(8,128)(2,1)S(1)} %shard_map.64) | data formatting | bytes 1048576

commit v4 on v3

v4 whole, which is shorter than its diff:
```python
import functools

import jax
import jax.numpy as jnp
from jax import lax
from jax.experimental import pallas as pl
from jax.experimental.pallas import tpu as pltpu
from jax.sharding import PartitionSpec as P

KB = 64
SEND_CAP = 2
HALVES = 2
LANES = 128
UNROLL = 64
MESH = pl.DeviceIdType.MESH


def repeat(count, body, init=None):
    if count <= UNROLL:
        for i in range(count):
            init = body(i, init)
        return init
    return lax.fori_loop(0, count, body, init)


def xor(value, mask):
    bit = 1
    while bit <= mask:
        if mask & bit:
            value = value + bit * (1 - 2 * lax.rem(lax.div(value, bit), 2))
        bit *= 2
    return value


def kernel(
    rows, cols, pos_in, hrow_in, keep_in, owner_in, p_ref, h_ref, out_ref,
    pos_ref, hrow_ref, keep_ref, owner_ref, pv, hown, hall, kept, outgoing, received, table, stable,
    local_sem, move_send, move_recv, core_send, core_recv, deal_send, deal_recv,
):
    me_r, me_c = lax.axis_index("row"), lax.axis_index("col")
    core = lax.rem(me_r, 2)
    listed_p = p_ref.shape[0]
    block = p_ref.shape[-1]
    rb, ncb = keep_ref.shape
    blocks = rb * ncb
    listed_h = hrow_ref.shape[0] // cols
    dims = rows.bit_length() - 2
    places = 2**dims
    power = cols & (cols - 1) == 0

    def target(step):
        return xor(me_c, step) if power else lax.rem(me_c + step, cols)

    def origin(step):
        return xor(me_c, step) if power else lax.rem(me_c + cols - step, cols)

    strides = []
    for i in range(dims):
        first, second = 2 ** (dims - i), 2 ** (i + 1)
        moves = [stride * (1 - 2 * lax.rem(lax.div(me_r, stride), 2)) for stride in (first, second)]
        strides.append(moves[0] + core * (moves[1] - moves[0]))
    pieces = [me_r]
    for stride in strides:
        pieces = pieces + [piece + stride for piece in pieces]
    partner = me_r + 1 - 2 * core
    half = block // HALVES
    left = lax.broadcasted_iota(jnp.int32, (block, block), 1) < half

    def swapped(tile):
        return pltpu.roll(tile, half, 1)

    def wide(tile):
        return tile.astype(jnp.float32)

    p_copy = pltpu.make_async_copy(p_ref, pv.at[pl.ds(0, listed_p)], local_sem.at[0])
    h_copy = pltpu.make_async_copy(h_ref, hown, local_sem.at[1])
    small = [
        pltpu.make_async_copy(given, held, local_sem.at[4 + i])
        for i, (given, held) in enumerate((
            (pos_in, pos_ref), (hrow_in, hrow_ref), (keep_in, keep_ref), (owner_in, owner_ref)
        ))
    ]
    h_copy.start()
    for copy in small:
        copy.start()

    barrier = pltpu.get_barrier_semaphore()
    for step in range(1, cols):
        pl.semaphore_signal(barrier, inc=1, device_id=(me_r, target(step)), device_id_type=MESH)
    for step in range(1, rows):
        pl.semaphore_signal(barrier, inc=1, device_id=(xor(me_r, step), me_c), device_id_type=MESH)
    p_copy.start()

    h_copy.wait()
    pairs = listed_h // 2
    halves = ([], [])
    for t in range(pairs):
        a, b = wide(hown[t]), wide(hown[pairs + t])
        halves[0].append(jnp.where(left, a, swapped(b)).astype(jnp.bfloat16))
        halves[1].append(jnp.where(left, swapped(a), b).astype(jnp.bfloat16))
    for k in range(HALVES):
        hall[k, me_c] = jnp.concatenate(halves[k], axis=0).reshape(hall.shape[2:])
    pl.semaphore_wait(barrier, cols + rows - 2)

    def first_copy(k, step):
        piece = hall.at[k, me_c, lax.div(me_r, 2), core]
        return pltpu.make_async_remote_copy(
            src_ref=piece, dst_ref=piece,
            send_sem=move_send.at[k * cols + step, 0], recv_sem=move_recv.at[k * cols + step, 0],
            device_id=(me_r, target(step)), device_id_type=MESH,
        )

    def plane_copy(k, step, place, onto):
        piece = hall.at[k, origin(step), lax.div(pieces[place], 2), core]
        return pltpu.make_async_remote_copy(
            src_ref=piece, dst_ref=piece,
            send_sem=move_send.at[k * cols + step, onto],
            recv_sem=move_recv.at[k * cols + step, onto],
            device_id=(pieces[onto], me_c), device_id_type=MESH,
        )

    def core_copy(k, step, side):
        held = hall.at[k, origin(step), :, side]
        return pltpu.make_async_remote_copy(
            src_ref=held, dst_ref=held,
            send_sem=core_send.at[k * cols + step], recv_sem=core_recv.at[k * cols + step],
            device_id=(partner, me_c), device_id_type=MESH,
        )

    for k in range(HALVES):
        for step in range(1, cols):
            first_copy(k, step).start()
    for copy in small:
        copy.wait()

    width = table.shape[-1]
    lane = lax.broadcasted_iota(jnp.int32, (8, width), 1)
    line = lax.broadcasted_iota(jnp.int32, (8, width), 0)
    wanted = repeat(
        hrow_ref.shape[0], lambda m, held: jnp.where(lane == m, hrow_ref[m], held),
        jnp.full((8, width), -1, jnp.int32),
    )
    wanted = jnp.where(wanted < 0, -1, wanted + line * KB)
    table[0] = repeat(
        listed_p, lambda q, held: jnp.where(wanted == pos_ref[q], q, held),
        jnp.full((8, width), listed_p, jnp.int32),
    )
    filled = jnp.full((8, width), blocks, jnp.int32)
    count = jnp.zeros((8, width), jnp.int32)
    for b in range(blocks):
        r, j = b // ncb, b % ncb
        hit = lane == owner_ref[r, 0, j]
        taken = jnp.where(keep_ref[r, j] == 1, b, blocks)
        filled = jnp.where(hit & (count == line), taken, filled)
        count = count + hit.astype(jnp.int32)
    table[1] = filled
    t_copy = pltpu.make_async_copy(table, stable, local_sem.at[2])
    t_copy.start()
    pv[listed_p] = jnp.zeros((block, block), jnp.bfloat16)
    for k in range(HALVES):
        for s in range(SEND_CAP):
            kept[k, s, blocks] = jnp.zeros((block, block), jnp.bfloat16)
    t_copy.wait()

    def multiply(k, column):
        panel = hall[k, column].reshape(pairs * block, block)
        parts = []
        for first in (0, pairs):
            sides = []
            for r in range(rb):
                sides.append(jnp.concatenate(
                    [pv[stable[0, r, column * listed_h + first + n]] for n in range(pairs)], axis=1
                ))
            parts.append(jnp.dot(
                jnp.concatenate(sides, axis=0), panel, preferred_element_type=jnp.float32
            ))
        for r in range(rb):
            low, high = [part[r * block:(r + 1) * block] for part in parts]
            total = jnp.where(left, low, high)
            total = total + swapped(total)
            zero = jnp.zeros_like(total)
            kept[k, 0, r * ncb + column] = jnp.where(left, total, zero).astype(jnp.bfloat16)
            kept[k, 1, r * ncb + column] = jnp.where(left, zero, total).astype(jnp.bfloat16)

    def deal_copy(k, step):
        owner = xor(me_r, step)
        return pltpu.make_async_remote_copy(
            src_ref=outgoing.at[k, owner], dst_ref=received.at[k, me_r],
            send_sem=deal_send.at[k * rows + step], recv_sem=deal_recv.at[k * rows + step],
            device_id=(owner, me_c), device_id_type=MESH,
        )

    def deal(k):
        for step in range(rows - 1, -1, -1):
            owner = xor(me_r, step)
            tile = kept[k, 0, stable[1, 0, owner]] + kept[k, 1, stable[1, 1, owner]]
            if step:
                outgoing[k, owner] = tile
                deal_copy(k, step).start()
            else:
                received[k, me_r] = tile

    for k in range(HALVES):
        for step in range(1, cols):
            first_copy(k, step).wait_recv()
            for place in range(places - 1, 0, -1):
                plane_copy(k, step, 0, place).start()
    p_copy.wait()
    for k in range(HALVES):
        multiply(k, me_c)
    for k in range(HALVES):
        for step in range(1, cols):
            for place in range(1, places):
                plane_copy(k, step, place, place).wait_recv()
            core_copy(k, step, core).start()
        for step in range(1, cols):
            core_copy(k, step, 1 - core).wait_recv()
            multiply(k, origin(step))
        deal(k)

    for k in range(HALVES):
        for step in range(1, cols):
            first_copy(k, step).wait_send()
            for place in range(1, places):
                plane_copy(k, step, 0, place).wait_send()
            core_copy(k, step, core).wait_send()
    for step in range(rows):
        sender = xor(me_r, step)
        if step:
            for k in range(HALVES):
                deal_copy(k, step).wait_send()
                deal_copy(k, step).wait_recv()
        a, b = wide(received[0, sender]), wide(received[1, sender])
        out_ref[sender, 0] = jnp.where(left, a, swapped(b)).astype(jnp.bfloat16)
        out_ref[sender, 1] = jnp.where(left, swapped(a), b).astype(jnp.bfloat16)


def local(rows, cols, p_blocks, p_positions, h_blocks, h_rows, keep_mask, owner_ids):
    listed_p, block = p_blocks.shape[:2]
    listed_h = h_blocks.shape[0]
    blocks = keep_mask.size
    depth = listed_h * block // rows // HALVES
    places = rows // 2
    width = -(-max(h_rows.shape[0], rows) // LANES) * LANES
    hbm = pl.BlockSpec(memory_space=pltpu.HBM)
    dma = pltpu.SemaphoreType.DMA
    return pl.pallas_call(
        functools.partial(kernel, rows, cols),
        out_shape=pltpu.VMEM((rows, SEND_CAP, block, block), jnp.bfloat16),
        in_specs=[hbm] * 6,
        out_specs=pl.BlockSpec(memory_space=pltpu.VMEM),
        scratch_shapes=[
            pltpu.SMEM(p_positions.shape, jnp.int32),
            pltpu.SMEM(h_rows.shape, jnp.int32),
            pltpu.SMEM(keep_mask.shape, jnp.int32),
            pltpu.SMEM((keep_mask.shape[0], 1, keep_mask.shape[1]), jnp.int32),
            pltpu.VMEM((listed_p + 1, block, block), jnp.bfloat16),
            pltpu.VMEM(h_blocks.shape, jnp.bfloat16),
            pltpu.VMEM((HALVES, cols, rows // 2, 2, depth, block), jnp.bfloat16),
            pltpu.VMEM((HALVES, SEND_CAP, blocks + 1, block, block), jnp.bfloat16),
            pltpu.VMEM((HALVES, rows, block, block), jnp.bfloat16),
            pltpu.VMEM((HALVES, rows, block, block), jnp.bfloat16),
            pltpu.VMEM((2, 8, width), jnp.int32),
            pltpu.SMEM((2, 8, width), jnp.int32),
            dma((8,)),
            dma((HALVES * cols, places)),
            dma((HALVES * cols, places)),
            dma((HALVES * cols,)),
            dma((HALVES * cols,)),
            dma((HALVES * rows,)),
            dma((HALVES * rows,)),
        ],
        compiler_params=pltpu.CompilerParams(
            collective_id=0, has_side_effects=True, vmem_limit_bytes=40 * 1024 * 1024
        ),
    )(*[
        pltpu.with_memory_space_constraint(given, pltpu.HBM) for given in (
            p_positions, h_rows, keep_mask, jnp.transpose(owner_ids, (0, 2, 1)), p_blocks,
            h_blocks,
        )
    ])


def solution(mesh):
    return jax.shard_map(
        functools.partial(local, mesh.shape["row"], mesh.shape["col"]),
        mesh=mesh,
        in_specs=(
            P(("row", "col"), None, None),
            P(("row", "col")),
            P("col", None, None),
            P(),
            P(("row", "col"), None),
            P(("row", "col"), None, None),
        ),
        out_specs=P(("row", "col"), None, None, None),
        check_vma=False,
    )
```

time: 24.9 us -> 24.8 us (level)
  no operation moved by 1% of the time
where the time goes in v4:
time: 24.8 us; the launch traced here: 24.6 us
  Pallas kernels  23.8 us (96%)
  local copies, waits for them, and re-layouts  0.8 us (3%)
    pallas_call x1, Pallas kernels, local(): pl.pallas_call(functools.partial(kernel, rows, cols), out_shape=pltpu.VME...  23.8 us
    unnamed x1, local copies, waits for them, and re-layouts  0.8 us

profile of v4, /device:TPU:0, one launch (start us, length us, event | category | flops | bytes accessed | tf_op | source)
XLA Modules:
  0.0 24.6 jit_solution(12158108248706060373)
XLA Ops:
  0.0 23.8 %shard_map.64 = bf16[8,2,128,128]{3,2,1,0:T(8,128)(2,1)S(1)} custom-call(s32[48]{0:T(128)} %pos_in.1, s32[32]{0:T(128)} %hrow_in.1, s32[2,4]{1,0:T(2,128)} %keep_in.1, s32[2,1,4]{2,1,0:T(1,128)} %bitcast.3, bf16[48,128,128]{2,1,0:T(8,128)(2,1)} %p_ref.1, bf16[8,128,128]{2,1,0:T(8,128)(2,1)} %h_ref.1), custom_call_target="tpu_custom_call" | custom-call | tf_op jit(solution)/shard_map/pallas_call | solution.py:247
  23.9 0.8 %copy.9 = bf16[8,2,128,128]{3,2,1,0:T(8,128)(2,1)} copy(bf16[8,2,128,128]{3,2,1,0:T(8,128)(2,1)S(1)} %shard_map.64) | data formatting | bytes 1048576

commit v5 on v4

--- a/solution.py
+++ b/solution.py
@@ -35,7 +35,7 @@
 def kernel(
     rows, cols, pos_in, hrow_in, keep_in, owner_in, p_ref, h_ref, out_ref,
     pos_ref, hrow_ref, keep_ref, owner_ref, pv, hown, hall, kept, outgoing, received, table, stable,
-    local_sem, move_send, move_recv, core_send, core_recv, deal_send, deal_recv,
+    local_sem, first_send, first_recv, plane_send, plane_recv, core_send, core_recv, deal_send, deal_recv,
 ):
     me_r, me_c = lax.axis_index("row"), lax.axis_index("col")
     core = lax.rem(me_r, 2)
@@ -44,8 +44,6 @@
     rb, ncb = keep_ref.shape
     blocks = rb * ncb
     listed_h = hrow_ref.shape[0] // cols
-    dims = rows.bit_length() - 2
-    places = 2**dims
     power = cols & (cols - 1) == 0
 
     def target(step):
@@ -54,14 +52,10 @@
     def origin(step):
         return xor(me_c, step) if power else lax.rem(me_c + cols - step, cols)
 
-    strides = []
-    for i in range(dims):
-        first, second = 2 ** (dims - i), 2 ** (i + 1)
-        moves = [stride * (1 - 2 * lax.rem(lax.div(me_r, stride), 2)) for stride in (first, second)]
-        strides.append(moves[0] + core * (moves[1] - moves[0]))
-    pieces = [me_r]
-    for stride in strides:
-        pieces = pieces + [piece + stride for piece in pieces]
+    sides = [lax.rem(lax.div(me_r, stride), 2) for stride in (rows // 2, 2)]
+    ways = [stride * (1 - 2 * side) for stride, side in zip((rows // 2, 2), sides)]
+    side = sides[0] + core * (sides[1] - sides[0])
+    friend = me_r + ways[0] + core * (ways[1] - ways[0])
     partner = me_r + 1 - 2 * core
     half = block // HALVES
     left = lax.broadcasted_iota(jnp.int32, (block, block), 1) < half
@@ -103,24 +97,23 @@
     pl.semaphore_wait(barrier, cols + rows - 2)
 
     def first_copy(k, step):
-        piece = hall.at[k, me_c, lax.div(me_r, 2), core]
+        piece = hall.at[k, me_c, side, core]
         return pltpu.make_async_remote_copy(
             src_ref=piece, dst_ref=piece,
-            send_sem=move_send.at[k * cols + step, 0], recv_sem=move_recv.at[k * cols + step, 0],
+            send_sem=first_send.at[k * cols + step], recv_sem=first_recv.at[k * cols + step],
             device_id=(me_r, target(step)), device_id_type=MESH,
         )
 
-    def plane_copy(k, step, place, onto):
-        piece = hall.at[k, origin(step), lax.div(pieces[place], 2), core]
+    def plane_copy(k, step, part):
+        piece = hall.at[k, origin(step), part, core]
         return pltpu.make_async_remote_copy(
             src_ref=piece, dst_ref=piece,
-            send_sem=move_send.at[k * cols + step, onto],
-            recv_sem=move_recv.at[k * cols + step, onto],
-            device_id=(pieces[onto], me_c), device_id_type=MESH,
-        )
-
-    def core_copy(k, step, side):
-        held = hall.at[k, origin(step), :, side]
+            send_sem=plane_send.at[k * cols + step], recv_sem=plane_recv.at[k * cols + step],
+            device_id=(friend, me_c), device_id_type=MESH,
+        )
+
+    def core_copy(k, step, part):
+        held = hall.at[k, origin(step), :, part]
         return pltpu.make_async_remote_copy(
             src_ref=held, dst_ref=held,
             send_sem=core_send.at[k * cols + step], recv_sem=core_recv.at[k * cols + step],
@@ -166,13 +159,13 @@
         panel = hall[k, column].reshape(pairs * block, block)
         parts = []
         for first in (0, pairs):
-            sides = []
+            lines = []
             for r in range(rb):
-                sides.append(jnp.concatenate(
+                lines.append(jnp.concatenate(
                     [pv[stable[0, r, column * listed_h + first + n]] for n in range(pairs)], axis=1
                 ))
             parts.append(jnp.dot(
-                jnp.concatenate(sides, axis=0), panel, preferred_element_type=jnp.float32
+                jnp.concatenate(lines, axis=0), panel, preferred_element_type=jnp.float32
             ))
         for r in range(rb):
             low, high = [part[r * block:(r + 1) * block] for part in parts]
@@ -203,15 +196,13 @@
     for k in range(HALVES):
         for step in range(1, cols):
             first_copy(k, step).wait_recv()
-            for place in range(places - 1, 0, -1):
-                plane_copy(k, step, 0, place).start()
+            plane_copy(k, step, side).start()
     p_copy.wait()
     for k in range(HALVES):
         multiply(k, me_c)
     for k in range(HALVES):
         for step in range(1, cols):
-            for place in range(1, places):
-                plane_copy(k, step, place, place).wait_recv()
+            plane_copy(k, step, 1 - side).wait_recv()
             core_copy(k, step, core).start()
         for step in range(1, cols):
             core_copy(k, step, 1 - core).wait_recv()
@@ -221,8 +212,7 @@
     for k in range(HALVES):
         for step in range(1, cols):
             first_copy(k, step).wait_send()
-            for place in range(1, places):
-                plane_copy(k, step, 0, place).wait_send()
+            plane_copy(k, step, side).wait_send()
             core_copy(k, step, core).wait_send()
     for step in range(rows):
         sender = xor(me_r, step)
@@ -239,8 +229,7 @@
     listed_p, block = p_blocks.shape[:2]
     listed_h = h_blocks.shape[0]
     blocks = keep_mask.size
-    depth = listed_h * block // rows // HALVES
-    places = rows // 2
+    depth = listed_h * block // HALVES // 4
     width = -(-max(h_rows.shape[0], rows) // LANES) * LANES
     hbm = pl.BlockSpec(memory_space=pltpu.HBM)
     dma = pltpu.SemaphoreType.DMA
@@ -256,15 +245,17 @@
             pltpu.SMEM((keep_mask.shape[0], 1, keep_mask.shape[1]), jnp.int32),
             pltpu.VMEM((listed_p + 1, block, block), jnp.bfloat16),
             pltpu.VMEM(h_blocks.shape, jnp.bfloat16),
-            pltpu.VMEM((HALVES, cols, rows // 2, 2, depth, block), jnp.bfloat16),
+            pltpu.VMEM((HALVES, cols, 2, 2, depth, block), jnp.bfloat16),
             pltpu.VMEM((HALVES, SEND_CAP, blocks + 1, block, block), jnp.bfloat16),
             pltpu.VMEM((HALVES, rows, block, block), jnp.bfloat16),
             pltpu.VMEM((HALVES, rows, block, block), jnp.bfloat16),
             pltpu.VMEM((2, 8, width), jnp.int32),
             pltpu.SMEM((2, 8, width), jnp.int32),
             dma((8,)),
-            dma((HALVES * cols, places)),
-            dma((HALVES * cols, places)),
+            dma((HALVES * cols,)),
+            dma((HALVES * cols,)),
+            dma((HALVES * cols,)),
+            dma((HALVES * cols,)),
             dma((HALVES * cols,)),
             dma((HALVES * cols,)),
             dma((HALVES * rows,)),

time: 24.8 us -> 25.2 us (1.016)
  Pallas kernels: 23.8 us -> 24.3 us
    pallas_call x1, Pallas kernels: 23.8 us -> 24.3 us  [local(): pl.pallas_call(functools.partial(kernel, rows, cols), out_shape=pltpu.VME...]
where the time goes in v5:
time: 25.2 us; the launch traced here: 25.1 us
  Pallas kernels  24.3 us (96%)
  local copies, waits for them, and re-layouts  0.8 us (3%)
    pallas_call x1, Pallas kernels, local(): pl.pallas_call(functools.partial(kernel, rows, cols), out_shape=pltpu.VME...  24.3 us
    unnamed x1, local copies, waits for them, and re-layouts  0.8 us

profile of v5, /device:TPU:0, one launch (start us, length us, event | category | flops | bytes accessed | tf_op | source)
XLA Modules:
  0.0 25.1 jit_solution(17628677173926291323)
XLA Ops:
  0.0 24.3 %shard_map.64 = bf16[8,2,128,128]{3,2,1,0:T(8,128)(2,1)S(1)} custom-call(s32[48]{0:T(128)} %pos_in.1, s32[32]{0:T(128)} %hrow_in.1, s32[2,4]{1,0:T(2,128)} %keep_in.1, s32[2,1,4]{2,1,0:T(1,128)} %bitcast.3, bf16[48,128,128]{2,1,0:T(8,128)(2,1)} %p_ref.1, bf16[8,128,128]{2,1,0:T(8,128)(2,1)} %h_ref.1), custom_call_target="tpu_custom_call" | custom-call | tf_op jit(solution)/shard_map/pallas_call | solution.py:236
  24.3 0.8 %copy.9 = bf16[8,2,128,128]{3,2,1,0:T(8,128)(2,1)} copy(bf16[8,2,128,128]{3,2,1,0:T(8,128)(2,1)S(1)} %shard_map.64) | data formatting | bytes 1048576

commit v6 on v3

--- a/solution.py
+++ b/solution.py
@@ -64,6 +64,12 @@
     toward = 1 - 2 * core
     partner = me_r + toward
 
+    barrier = pltpu.get_barrier_semaphore()
+    for step in range(1, cols):
+        pl.semaphore_signal(barrier, inc=1, device_id=(me_r, target(step)), device_id_type=MESH)
+    for step in range(1, rows):
+        pl.semaphore_signal(barrier, inc=1, device_id=(xor(me_r, step), me_c), device_id_type=MESH)
+
     p_copy = pltpu.make_async_copy(p_ref, pv.at[pl.ds(0, listed_p)], local_sem.at[0])
     h_copy = pltpu.make_async_copy(h_ref, hall.at[me_c], local_sem.at[1])
     small = [
@@ -74,33 +80,32 @@
     ]
     for copy in small:
         copy.start()
-
-    barrier = pltpu.get_barrier_semaphore()
-    for step in range(1, cols):
-        pl.semaphore_signal(barrier, inc=1, device_id=(me_r, target(step)), device_id_type=MESH)
-    for step in range(1, rows):
-        pl.semaphore_signal(barrier, inc=1, device_id=(xor(me_r, step), me_c), device_id_type=MESH)
     h_copy.start()
     p_copy.start()
     pl.semaphore_wait(barrier, cols + rows - 2)
 
     def first_copy(step):
         return pltpu.make_async_remote_copy(
-            src_ref=h_ref.at[me_r], dst_ref=hall.at[me_c, me_r],
+            src_ref=h_ref.at[lax.div(me_r, 2), core], dst_ref=hall.at[me_c, lax.div(me_r, 2), core],
             send_sem=move_send.at[step, 0], recv_sem=move_recv.at[step, 0],
             device_id=(me_r, target(step)), device_id_type=MESH,
         )
 
     def plane_copy(step, place, onto, to_row, sends, recvs):
-        piece = hall.at[origin(step), pieces[place]]
+        piece = hall.at[origin(step), lax.div(pieces[place], 2), core]
         return pltpu.make_async_remote_copy(
             src_ref=piece, dst_ref=piece,
             send_sem=sends.at[step, onto], recv_sem=recvs.at[step, onto],
             device_id=(to_row, me_c), device_id_type=MESH,
         )
 
-    def core_copy(step, place):
-        return plane_copy(step, place, place, partner, core_send, core_recv)
+    def core_copy(step, side):
+        held = hall.at[origin(step), :, side]
+        return pltpu.make_async_remote_copy(
+            src_ref=held, dst_ref=held,
+            send_sem=core_send.at[step], recv_sem=core_recv.at[step],
+            device_id=(partner, me_c), device_id_type=MESH,
+        )
 
     for step in range(1, cols):
         first_copy(step).start()
@@ -115,30 +120,29 @@
         jnp.full((8, width), -1, jnp.int32),
     )
     wanted = jnp.where(wanted < 0, -1, wanted + line * KB)
-    table[0] = repeat(
+    found = repeat(
         listed_p, lambda q, held: jnp.where(wanted == pos_ref[q], q, held),
         jnp.full((8, width), listed_p, jnp.int32),
     )
     filled = jnp.full((8, width), blocks, jnp.int32)
-    count = jnp.zeros((8, width), jnp.int32)
+    count = jnp.zeros((8, width), jnp.int32) + rb
     for b in range(blocks):
         r, j = b // ncb, b % ncb
         hit = lane == owner_ref[r, 0, j]
         taken = jnp.where(keep_ref[r, j] == 1, b, blocks)
         filled = jnp.where(hit & (count == line), taken, filled)
         count = count + hit.astype(jnp.int32)
-    table[1] = filled
+    table[...] = jnp.where(line < rb, found, filled)
     t_copy = pltpu.make_async_copy(table, stable, local_sem.at[2])
     t_copy.start()
     pv[listed_p] = jnp.zeros((block, block), jnp.bfloat16)
     kept[blocks] = jnp.zeros((block, block), jnp.bfloat16)
-    t_copy.wait()
 
     def multiply(column):
         sides = []
         for r in range(rb):
             sides.append(jnp.concatenate(
-                [pv[stable[0, r, column * listed_h + n]] for n in range(listed_h)], axis=1
+                [pv[stable[r, column * listed_h + n]] for n in range(listed_h)], axis=1
             ))
         panel = hall[column].reshape(listed_h * block, block)
         product = jnp.dot(
@@ -151,23 +155,18 @@
         first_copy(step).wait_recv()
         for place in range(places - 1, 0, -1):
             plane_copy(step, 0, place, pieces[place], move_send, move_recv).start()
-        core_copy(step, 0).start()
+    t_copy.wait()
     p_copy.wait()
     h_copy.wait()
     multiply(me_c)
-    for step in range(1, cols):
-        for place in range(1, places):
-            plane_copy(step, place, place, me_r, move_send, move_recv).wait_recv()
-            core_copy(step, place).start()
-    for step in range(1, cols):
-        for place in range(places):
-            other = pieces[place] + toward
-            pltpu.make_async_remote_copy(
-                src_ref=hall.at[origin(step), other], dst_ref=hall.at[origin(step), other],
-                send_sem=core_send.at[step, place], recv_sem=core_recv.at[step, place],
-                device_id=(partner, me_c), device_id_type=MESH,
-            ).wait_recv()
-        multiply(origin(step))
+    for step in range(1, cols + 2):
+        if step < cols:
+            for place in range(1, places):
+                plane_copy(step, place, place, me_r, move_send, move_recv).wait_recv()
+            core_copy(step, core).start()
+        if step > 2:
+            core_copy(step - 2, 1 - core).wait_recv()
+            multiply(origin(step - 2))
 
     def deal(step):
         owner = xor(me_r, step)
@@ -180,17 +179,16 @@
     for step in range(rows - 1, -1, -1):
         owner = xor(me_r, step)
         for s in range(SEND_CAP):
-            outgoing[owner, s] = kept[stable[1, s, owner]]
+            outgoing[owner, s] = kept[stable[rb + s, owner]]
         if step:
             deal(step).start()
     own = pltpu.make_async_copy(outgoing.at[me_r], out_ref.at[me_r], local_sem.at[3])
     own.start()
     for step in range(1, cols):
         first_copy(step).wait_send()
-        for place in range(places):
-            if place:
-                plane_copy(step, 0, place, me_r, move_send, move_recv).wait_send()
-            core_copy(step, place).wait_send()
+        for place in range(1, places):
+            plane_copy(step, 0, place, me_r, move_send, move_recv).wait_send()
+        core_copy(step, core).wait_send()
     for step in range(rows - 1, 0, -1):
         deal(step).wait_send()
         deal(step).wait_recv()
@@ -218,16 +216,16 @@
             pltpu.SMEM(keep_mask.shape, jnp.int32),
             pltpu.SMEM((keep_mask.shape[0], 1, keep_mask.shape[1]), jnp.int32),
             pltpu.VMEM((listed_p + 1, block, block), jnp.bfloat16),
-            pltpu.VMEM((cols, rows, depth, block), jnp.bfloat16),
+            pltpu.VMEM((cols, rows // 2, 2, depth, block), jnp.bfloat16),
             pltpu.VMEM((blocks + 1, block, block), jnp.bfloat16),
             pltpu.VMEM((rows, SEND_CAP, block, block), jnp.bfloat16),
-            pltpu.VMEM((2, 8, width), jnp.int32),
-            pltpu.SMEM((2, 8, width), jnp.int32),
+            pltpu.VMEM((8, width), jnp.int32),
+            pltpu.SMEM((8, width), jnp.int32),
             dma((8,)),
             dma((cols, places)),
             dma((cols, places)),
-            dma((cols, places)),
-            dma((cols, places)),
+            dma((cols,)),
+            dma((cols,)),
             dma((rows,)),
             dma((rows,)),
         ],
@@ -237,7 +235,7 @@
     )(*[
         pltpu.with_memory_space_constraint(given, pltpu.HBM) for given in (
             p_positions, h_rows, keep_mask, jnp.transpose(owner_ids, (0, 2, 1)), p_blocks,
-            h_blocks.reshape(rows, depth, block),
+            h_blocks.reshape(rows // 2, 2, depth, block),
         )
     ])
 

time: 24.9 us -> 24.6 us (0.988)
  Pallas kernels: 24 us -> 23.6 us
    pallas_call x1, Pallas kernels: 24 us -> 23.6 us  [local(): pl.pallas_call(functools.partial(kernel, rows, cols), out_shape=pltpu.VME...]
where the time goes in v6:
time: 24.6 us; the launch traced here: 24.5 us
  Pallas kernels  23.6 us (96%)
  local copies, waits for them, and re-layouts  0.8 us (3%)
    pallas_call x1, Pallas kernels, local(): pl.pallas_call(functools.partial(kernel, rows, cols), out_shape=pltpu.VME...  23.6 us
    unnamed x1, local copies, waits for them, and re-layouts  0.8 us

profile of v6, /device:TPU:0, one launch (start us, length us, event | category | flops | bytes accessed | tf_op | source)
XLA Modules:
  0.0 24.5 jit_solution(112357052271786362)
XLA Ops:
  0.0 23.6 %shard_map.64 = bf16[8,2,128,128]{3,2,1,0:T(8,128)(2,1)S(1)} custom-call(s32[48]{0:T(128)} %pos_in.1, s32[32]{0:T(128)} %hrow_in.1, s32[2,4]{1,0:T(2,128)} %keep_in.1, s32[2,1,4]{2,1,0:T(1,128)} %bitcast.5, bf16[48,128,128]{2,1,0:T(8,128)(2,1)} %p_ref.1, bf16[4,2,128,128]{3,2,1,0:T(8,128)(2,1)} %bitcast.4), custom_call_target="tpu_custom_call" | custom-call | tf_op jit(solution)/shard_map/pallas_call | solution.py:208
  23.7 0.8 %copy.9 = bf16[8,2,128,128]{3,2,1,0:T(8,128)(2,1)} copy(bf16[8,2,128,128]{3,2,1,0:T(8,128)(2,1)S(1)} %shard_map.64) | data formatting | bytes 1048576

commit v7 on v6

--- a/solution.py
+++ b/solution.py
@@ -34,7 +34,7 @@
 def kernel(
     rows, cols, pos_in, hrow_in, keep_in, owner_in, p_ref, h_ref, out_ref,
     pos_ref, hrow_ref, keep_ref, owner_ref, pv, hall, kept, outgoing, table, stable,
-    local_sem, move_send, move_recv, core_send, core_recv, deal_send, deal_recv,
+    local_sem, first_send, move_send, move_recv, core_send, core_recv, deal_send, deal_recv,
 ):
     me_r, me_c = lax.axis_index("row"), lax.axis_index("col")
     core = lax.rem(me_r, 2)
@@ -45,13 +45,13 @@
     listed_h = hrow_ref.shape[0] // cols
     dims = rows.bit_length() - 2
     places = 2**dims
-    power = cols & (cols - 1) == 0
-
-    def target(step):
-        return xor(me_c, step) if power else lax.rem(me_c + step, cols)
-
-    def origin(step):
-        return xor(me_c, step) if power else lax.rem(me_c + cols - step, cols)
+    before, after = me_c > 0, me_c < cols - 1
+    near = jnp.minimum(me_c, cols - 1 - me_c)
+    far_way = jnp.where(me_c > cols - 1 - me_c, -1, 1)
+    origins = [me_c]
+    for step in range(1, cols):
+        close = (step + 1) // 2 * (1 if step % 2 else -1)
+        origins.append(me_c + jnp.where(step <= 2 * near, close, far_way * (step - near)))
 
     strides = []
     for i in range(dims):
@@ -65,8 +65,11 @@
     partner = me_r + toward
 
     barrier = pltpu.get_barrier_semaphore()
-    for step in range(1, cols):
-        pl.semaphore_signal(barrier, inc=1, device_id=(me_r, target(step)), device_id_type=MESH)
+    for exists, way in ((before, -1), (after, 1)):
+        @pl.when(exists)
+        def _():
+            pl.semaphore_signal(barrier, inc=1, device_id=(me_r, me_c + way), device_id_type=MESH)
+
     for step in range(1, rows):
         pl.semaphore_signal(barrier, inc=1, device_id=(xor(me_r, step), me_c), device_id_type=MESH)
 
@@ -82,33 +85,48 @@
         copy.start()
     h_copy.start()
     p_copy.start()
-    pl.semaphore_wait(barrier, cols + rows - 2)
-
-    def first_copy(step):
+    pl.semaphore_wait(barrier, rows - 1 + jnp.minimum(me_c, 1) + jnp.minimum(cols - 1 - me_c, 1))
+
+    def first_copy(way):
         return pltpu.make_async_remote_copy(
             src_ref=h_ref.at[lax.div(me_r, 2), core], dst_ref=hall.at[me_c, lax.div(me_r, 2), core],
-            send_sem=move_send.at[step, 0], recv_sem=move_recv.at[step, 0],
-            device_id=(me_r, target(step)), device_id_type=MESH,
-        )
+            send_sem=first_send.at[(way + 1) // 2], recv_sem=move_recv.at[me_c, 0],
+            device_id=(me_r, me_c + way), device_id_type=MESH,
+        )
+
+    def relay_copy(step):
+        from_panel = origins[step]
+        piece = hall.at[from_panel, lax.div(me_r, 2), core]
+        return pltpu.make_async_remote_copy(
+            src_ref=piece, dst_ref=piece,
+            send_sem=move_send.at[from_panel, 0], recv_sem=move_recv.at[from_panel, 0],
+            device_id=(me_r, me_c + jnp.where(from_panel < me_c, 1, -1)), device_id_type=MESH,
+        )
+
+    def passes(step):
+        return ((origins[step] < me_c) & after) | ((origins[step] > me_c) & before)
 
     def plane_copy(step, place, onto, to_row, sends, recvs):
-        piece = hall.at[origin(step), lax.div(pieces[place], 2), core]
+        piece = hall.at[origins[step], lax.div(pieces[place], 2), core]
         return pltpu.make_async_remote_copy(
             src_ref=piece, dst_ref=piece,
-            send_sem=sends.at[step, onto], recv_sem=recvs.at[step, onto],
+            send_sem=sends.at[origins[step], onto], recv_sem=recvs.at[origins[step], onto],
             device_id=(to_row, me_c), device_id_type=MESH,
         )
 
     def core_copy(step, side):
-        held = hall.at[origin(step), :, side]
+        held = hall.at[origins[step], :, side]
         return pltpu.make_async_remote_copy(
             src_ref=held, dst_ref=held,
-            send_sem=core_send.at[step], recv_sem=core_recv.at[step],
+            send_sem=core_send.at[origins[step]], recv_sem=core_recv.at[origins[step]],
             device_id=(partner, me_c), device_id_type=MESH,
         )
 
-    for step in range(1, cols):
-        first_copy(step).start()
+    for exists, way in ((before, -1), (after, 1)):
+        @pl.when(exists)
+        def _():
+            first_copy(way).start()
+
     for copy in small:
         copy.wait()
 
@@ -152,7 +170,12 @@
             kept[r * ncb + column] = product[r * block:(r + 1) * block]
 
     for step in range(1, cols):
-        first_copy(step).wait_recv()
+        relay_copy(step).wait_recv()
+
+        @pl.when(passes(step))
+        def _():
+            relay_copy(step).start()
+
         for place in range(places - 1, 0, -1):
             plane_copy(step, 0, place, pieces[place], move_send, move_recv).start()
     t_copy.wait()
@@ -166,7 +189,7 @@
             core_copy(step, core).start()
         if step > 2:
             core_copy(step - 2, 1 - core).wait_recv()
-            multiply(origin(step - 2))
+            multiply(origins[step - 2])
 
     def deal(step):
         owner = xor(me_r, step)
@@ -184,8 +207,16 @@
             deal(step).start()
     own = pltpu.make_async_copy(outgoing.at[me_r], out_ref.at[me_r], local_sem.at[3])
     own.start()
+    for exists, way in ((before, -1), (after, 1)):
+        @pl.when(exists)
+        def _():
+            first_copy(way).wait_send()
+
     for step in range(1, cols):
-        first_copy(step).wait_send()
+        @pl.when(passes(step))
+        def _():
+            relay_copy(step).wait_send()
+
         for place in range(1, places):
             plane_copy(step, 0, place, me_r, move_send, move_recv).wait_send()
         core_copy(step, core).wait_send()
@@ -222,6 +253,7 @@
             pltpu.VMEM((8, width), jnp.int32),
             pltpu.SMEM((8, width), jnp.int32),
             dma((8,)),
+            dma((2,)),
             dma((cols, places)),
             dma((cols, places)),
             dma((cols,)),

time: 24.6 us -> 28.3 us (1.15)
  Pallas kernels: 23.6 us -> 27.4 us
    pallas_call x1, Pallas kernels: 23.6 us -> 27.4 us  [local(): pl.pallas_call(functools.partial(kernel, rows, cols), out_shape=pltpu.VME...]
where the time goes in v7:
time: 28.3 us; the launch traced here: 28.2 us
  Pallas kernels  27.4 us (97%)
  local copies, waits for them, and re-layouts  0.8 us (3%)
    pallas_call x1, Pallas kernels, local(): pl.pallas_call(functools.partial(kernel, rows, cols), out_shape=pltpu.VME...  27.4 us
    unnamed x1, local copies, waits for them, and re-layouts  0.8 us

profile of v7, /device:TPU:0, one launch (start us, length us, event | category | flops | bytes accessed | tf_op | source)
XLA Modules:
  0.0 28.2 jit_solution(7032996725218112956)
XLA Ops:
  0.0 27.4 %shard_map.64 = bf16[8,2,128,128]{3,2,1,0:T(8,128)(2,1)S(1)} custom-call(s32[48]{0:T(128)} %pos_in.1, s32[32]{0:T(128)} %hrow_in.1, s32[2,4]{1,0:T(2,128)} %keep_in.1, s32[2,1,4]{2,1,0:T(1,128)} %bitcast.5, bf16[48,128,128]{2,1,0:T(8,128)(2,1)} %p_ref.1, bf16[4,2,128,128]{3,2,1,0:T(8,128)(2,1)} %bitcast.4), custom_call_target="tpu_custom_call" | custom-call | tf_op jit(solution)/shard_map/pallas_call | solution.py:239
  27.4 0.8 %copy.9 = bf16[8,2,128,128]{3,2,1,0:T(8,128)(2,1)} copy(bf16[8,2,128,128]{3,2,1,0:T(8,128)(2,1)S(1)} %shard_map.64) | data formatting | bytes 1048576

commit v8 on v4

--- a/solution.py
+++ b/solution.py
@@ -63,6 +63,12 @@
     for stride in strides:
         pieces = pieces + [piece + stride for piece in pieces]
     partner = me_r + 1 - 2 * core
+    barrier = pltpu.get_barrier_semaphore()
+    for step in range(1, cols):
+        pl.semaphore_signal(barrier, inc=1, device_id=(me_r, target(step)), device_id_type=MESH)
+    for step in range(1, rows):
+        pl.semaphore_signal(barrier, inc=1, device_id=(xor(me_r, step), me_c), device_id_type=MESH)
+
     half = block // HALVES
     left = lax.broadcasted_iota(jnp.int32, (block, block), 1) < half
 
@@ -83,12 +89,6 @@
     h_copy.start()
     for copy in small:
         copy.start()
-
-    barrier = pltpu.get_barrier_semaphore()
-    for step in range(1, cols):
-        pl.semaphore_signal(barrier, inc=1, device_id=(me_r, target(step)), device_id_type=MESH)
-    for step in range(1, rows):
-        pl.semaphore_signal(barrier, inc=1, device_id=(xor(me_r, step), me_c), device_id_type=MESH)
     p_copy.start()
 
     h_copy.wait()
@@ -141,26 +141,25 @@
         jnp.full((8, width), -1, jnp.int32),
     )
     wanted = jnp.where(wanted < 0, -1, wanted + line * KB)
-    table[0] = repeat(
+    found = repeat(
         listed_p, lambda q, held: jnp.where(wanted == pos_ref[q], q, held),
         jnp.full((8, width), listed_p, jnp.int32),
     )
     filled = jnp.full((8, width), blocks, jnp.int32)
-    count = jnp.zeros((8, width), jnp.int32)
+    count = jnp.zeros((8, width), jnp.int32) + rb
     for b in range(blocks):
         r, j = b // ncb, b % ncb
         hit = lane == owner_ref[r, 0, j]
         taken = jnp.where(keep_ref[r, j] == 1, b, blocks)
         filled = jnp.where(hit & (count == line), taken, filled)
         count = count + hit.astype(jnp.int32)
-    table[1] = filled
+    table[...] = jnp.where(line < rb, found, filled)
     t_copy = pltpu.make_async_copy(table, stable, local_sem.at[2])
     t_copy.start()
     pv[listed_p] = jnp.zeros((block, block), jnp.bfloat16)
     for k in range(HALVES):
         for s in range(SEND_CAP):
             kept[k, s, blocks] = jnp.zeros((block, block), jnp.bfloat16)
-    t_copy.wait()
 
     def multiply(k, column):
         panel = hall[k, column].reshape(pairs * block, block)
@@ -169,7 +168,7 @@
             sides = []
             for r in range(rb):
                 sides.append(jnp.concatenate(
-                    [pv[stable[0, r, column * listed_h + first + n]] for n in range(pairs)], axis=1
+                    [pv[stable[r, column * listed_h + first + n]] for n in range(pairs)], axis=1
                 ))
             parts.append(jnp.dot(
                 jnp.concatenate(sides, axis=0), panel, preferred_element_type=jnp.float32
@@ -193,7 +192,7 @@
     def deal(k):
         for step in range(rows - 1, -1, -1):
             owner = xor(me_r, step)
-            tile = kept[k, 0, stable[1, 0, owner]] + kept[k, 1, stable[1, 1, owner]]
+            tile = kept[k, 0, stable[rb, owner]] + kept[k, 1, stable[rb + 1, owner]]
             if step:
                 outgoing[k, owner] = tile
                 deal_copy(k, step).start()
@@ -205,6 +204,7 @@
             first_copy(k, step).wait_recv()
             for place in range(places - 1, 0, -1):
                 plane_copy(k, step, 0, place).start()
+    t_copy.wait()
     p_copy.wait()
     for k in range(HALVES):
         multiply(k, me_c)
@@ -213,6 +213,7 @@
             for place in range(1, places):
                 plane_copy(k, step, place, place).wait_recv()
             core_copy(k, step, core).start()
+    for k in range(HALVES):
         for step in range(1, cols):
             core_copy(k, step, 1 - core).wait_recv()
             multiply(k, origin(step))
@@ -260,8 +261,8 @@
             pltpu.VMEM((HALVES, SEND_CAP, blocks + 1, block, block), jnp.bfloat16),
             pltpu.VMEM((HALVES, rows, block, block), jnp.bfloat16),
             pltpu.VMEM((HALVES, rows, block, block), jnp.bfloat16),
-            pltpu.VMEM((2, 8, width), jnp.int32),
-            pltpu.SMEM((2, 8, width), jnp.int32),
+            pltpu.VMEM((8, width), jnp.int32),
+            pltpu.SMEM((8, width), jnp.int32),
             dma((8,)),
             dma((HALVES * cols, places)),
             dma((HALVES * cols, places)),

time: 24.8 us -> 24.7 us (level)
  no operation moved by 1% of the time
where the time goes in v8:
time: 24.7 us; the launch traced here: 24.6 us
  Pallas kernels  23.8 us (96%)
  local copies, waits for them, and re-layouts  0.8 us (3%)
    pallas_call x1, Pallas kernels, local(): pl.pallas_call(functools.partial(kernel, rows, cols), out_shape=pltpu.VME...  23.8 us
    unnamed x1, local copies, waits for them, and re-layouts  0.8 us

profile of v8, /device:TPU:0, one launch (start us, length us, event | category | flops | bytes accessed | tf_op | source)
XLA Modules:
  0.0 24.6 jit_solution(6453815754069232265)
XLA Ops:
  0.0 23.8 %shard_map.64 = bf16[8,2,128,128]{3,2,1,0:T(8,128)(2,1)S(1)} custom-call(s32[48]{0:T(128)} %pos_in.1, s32[32]{0:T(128)} %hrow_in.1, s32[2,4]{1,0:T(2,128)} %keep_in.1, s32[2,1,4]{2,1,0:T(1,128)} %bitcast.3, bf16[48,128,128]{2,1,0:T(8,128)(2,1)} %p_ref.1, bf16[8,128,128]{2,1,0:T(8,128)(2,1)} %h_ref.1), custom_call_target="tpu_custom_call" | custom-call | tf_op jit(solution)/shard_map/pallas_call | solution.py:248
  23.8 0.8 %copy.9 = bf16[8,2,128,128]{3,2,1,0:T(8,128)(2,1)} copy(bf16[8,2,128,128]{3,2,1,0:T(8,128)(2,1)S(1)} %shard_map.64) | data formatting | bytes 1048576

commit v9 on v6

--- a/solution.py
+++ b/solution.py
@@ -107,7 +107,7 @@
             device_id=(partner, me_c), device_id_type=MESH,
         )
 
-    for step in range(1, cols):
+    for step in range(cols - 1, 0, -1):
         first_copy(step).start()
     for copy in small:
         copy.wait()

time: 24.6 us -> 25 us (1.016)
  Pallas kernels: 23.6 us -> 24 us
    pallas_call x1, Pallas kernels: 23.6 us -> 24 us  [local(): pl.pallas_call(functools.partial(kernel, rows, cols), out_shape=pltpu.VME...]
where the time goes in v9:
time: 25 us; the launch traced here: 24.8 us
  Pallas kernels  24 us (96%)
  local copies, waits for them, and re-layouts  0.8 us (3%)
    pallas_call x1, Pallas kernels, local(): pl.pallas_call(functools.partial(kernel, rows, cols), out_shape=pltpu.VME...  24 us
    unnamed x1, local copies, waits for them, and re-layouts  0.8 us

profile of v9, /device:TPU:0, one launch (start us, length us, event | category | flops | bytes accessed | tf_op | source)
XLA Modules:
  0.0 24.8 jit_solution(6533116519657634680)
XLA Ops:
  0.0 24.0 %shard_map.64 = bf16[8,2,128,128]{3,2,1,0:T(8,128)(2,1)S(1)} custom-call(s32[48]{0:T(128)} %pos_in.1, s32[32]{0:T(128)} %hrow_in.1, s32[2,4]{1,0:T(2,128)} %keep_in.1, s32[2,1,4]{2,1,0:T(1,128)} %bitcast.5, bf16[48,128,128]{2,1,0:T(8,128)(2,1)} %p_ref.1, bf16[4,2,128,128]{3,2,1,0:T(8,128)(2,1)} %bitcast.4), custom_call_target="tpu_custom_call" | custom-call | tf_op jit(solution)/shard_map/pallas_call | solution.py:208
  24.1 0.8 %copy.9 = bf16[8,2,128,128]{3,2,1,0:T(8,128)(2,1)} copy(bf16[8,2,128,128]{3,2,1,0:T(8,128)(2,1)S(1)} %shard_map.64) | data formatting | bytes 1048576
